TPU v7x, 32 devices: a whole 2x2x4 slice. The times are simulated.
32 devices in a mesh: sec: 4 (over y, x), own: 8 (over z, core).
Axes of the slice: x: 2, y: 2, z: 4, core: 2. Of those that a mesh axis runs over, the one named last changes fastest.
Arguments:
- right_sides: float32 [2, 128, 8192], P(None, None, ('sec', 'own')), may hold values from -6 to 6
- inv_diag: float32 [8192, 256], P(('sec', 'own')), may hold values from -1 to 2, as said below
- factor_tiles: bfloat16 [8192, 2048], P(('sec', 'own')), may hold values from -0.0625 to 0.0625
- structure: int32 [32, 8], P(('sec', 'own')), may hold values 0 or 1
- ancestor: int32 [4, 8], P('sec'), may hold values from 0 to 7, each once within a row
- carried: float32 [128, 8192], P(None, ('sec', 'own')), may hold values from -4 to 4
Outputs:
- solution: float32 [2, 128, 8192], P(None, None, ('sec', 'own'))
- carry_out: float32 [128, 8192], P(None, ('sec', 'own'))
Inputs may be any that keep to these rules, and one draw needn't show every extreme that they name: `inv_diag`: each diagonal block is the identity plus a dense part of moderate size. `ancestor`: each row is a permutation of 0 to 7.
All inputs are finite; a program needn't handle non-finite values. No bound on the sum of `structure` on one device may be relied on, other than what follows from the above.
Results may differ from a plain program's by a relative error of at most 0.0003.
Values sent between devices are 32-bit elements; how exact they have to be, the bound alone decides.
A program may use at most 64 MiB of HBM per device.

v0:
```python
import jax
import jax.numpy as jnp
from jax import lax
from jax.sharding import PartitionSpec as P


def passed_along(value, axis, by):
    peers = lax.axis_size(axis)
    pairs = [(i, i + by) for i in range(peers) if 0 <= i + by < peers]
    return lax.ppermute(value, axis, pairs)


def shards(right_sides, inv_diag, factor_tiles, structure, ancestor, carried):
    highest = lax.Precision.HIGHEST
    block_rows = inv_diag.shape[1]
    slots = structure.shape[1]
    selector = structure[0].astype(jnp.float32)[:, None] * (
        ancestor[0][:, None] == jnp.arange(slots, dtype=jnp.int32)[None, :]
    ).astype(jnp.float32)
    wide_tiles = factor_tiles.astype(jnp.float32).reshape(block_rows, slots, block_rows)
    routed_tiles = jnp.einsum("iab,aj->ijb", wide_tiles, selector, precision=highest).reshape(
        block_rows, slots * block_rows
    )
    incoming = carried
    solved_all = []
    for tick_index in range(right_sides.shape[0]):
        solved = jnp.dot(
            right_sides[tick_index] - incoming,
            inv_diag,
            precision=highest,
            preferred_element_type=jnp.float32,
        )
        solved_all.append(solved)
        routed = jnp.dot(
            solved, routed_tiles, precision=highest, preferred_element_type=jnp.float32
        )
        summed = lax.psum_scatter(routed, "own", scatter_dimension=1, tiled=True)
        incoming = passed_along(summed, "sec", 1)
    return (jnp.stack(solved_all), incoming)


def solution(mesh):
    in_specs = (
        P(None, None, ("sec", "own")),
        P(("sec", "own"), None),
        P(("sec", "own"), None),
        P(("sec", "own"), None),
        P("sec", None),
        P(None, ("sec", "own")),
    )
    out_specs = (P(None, None, ("sec", "own")), P(None, ("sec", "own")))
    return jax.shard_map(shards, mesh=mesh, in_specs=in_specs, out_specs=out_specs, check_vma=False)
```

profile of v0, /device:TPU:4, one launch (start us, length us, event | category | flops | bytes accessed | tf_op | source)
XLA Modules:
  0.0 102.8 jit_solution(16538200196288220277)
XLA Ops:
  7.2 0.0 copy-start
  7.2 0.0 copy-start.4
  7.2 0.0 copy-start.3
  7.2 0.0 reduce-scatter.3.cloned.1.call-start
  7.2 1.6 %copy.8 = bf16[32,8,8,256]{3,2,1,0:T(8,128)(2,1)S(1)} copy(bf16[32,8,8,256]{3,1,2,0:T(8,128)(2,1)} %bitcast.32) | data formatting | bytes 2097152
  8.8 0.0 copy-done.4
  8.8 0.0 copy-done.3
  8.8 1.0 fusion.4
  9.8 0.0 copy-start.1
  9.9 0.0 copy-start.2
  9.9 0.9 copy.9
  10.8 0.0 copy-done
  10.8 0.0 copy-done.1
  10.8 0.0 copy-done.2
  10.8 0.3 fusion.1
  11.1 2.2 %fusion.11 = f32[128,2048]{1,0:T(8,128)} fusion(f32[128,256]{1,0:T(8,128)S(1)} %fusion.1, f32[256,2048]{1,0:T(8,128)S(1)} %bitcast.26), kind=kOutput, calls=%fused_computation.16 | convolution fusion | flops 805306368 | bytes 3276800 | tf_op jit(solution)/shard_map/dot_general | solution.py:34
  13.3 0.0 reduce-scatter.3.cloned.1.call-update
  13.4 0.0 reduce-scatter.5.cloned.1.call-start
  13.4 33.7 %reduce-scatter.3.cloned.1.call-done = f32[128,256]{1,0:T(8,128)} async-done(((f32[128,2048]{1,0:T(8,128)}), f32[128,256]{1,0:T(8,128)}) %reduce-scatter.3.cloned.1.call-update) | async-done | bytes 131088 | tf_op jit(solution)/shard_map/reduce_scatter | solution.py:37
  47.1 3.4 %collective-permute-start = (f32[128,256]{1,0:T(8,128)}, f32[128,256]{1,0:T(8,128)S(1)}, u32[]{:S(2)}, u32[]{:S(2)}) collective-permute-start(f32[128,256]{1,0:T(8,128)} %reduce-scatter.3.cloned.1.call-done), channel_id=1, source_target_pairs={{0,8},{8,16},{16,24},{1,9},{9,17},{17,25},{2,10},{10,18},{18,26},{... | collective-permute-start | bytes 393224 | tf_op jit(solution)/shard_map/ppermute | solution.py:10
  50.4 4.6 %collective-permute-done = f32[128,256]{1,0:T(8,128)S(1)} collective-permute-done((f32[128,256]{1,0:T(8,128)}, f32[128,256]{1,0:T(8,128)S(1)}, u32[]{:S(2)}, u32[]{:S(2)}) %collective-permute-start) | collective-permute-done | bytes 131104 | tf_op jit(solution)/shard_map/ppermute | solution.py:10
  55.0 0.3 fusion
  55.3 2.2 %fusion.12 = f32[128,2048]{1,0:T(8,128)} fusion(f32[128,256]{1,0:T(8,128)S(1)} %fusion, f32[256,2048]{1,0:T(8,128)S(1)} %bitcast.27), kind=kOutput, calls=%fused_computation.17 | convolution fusion | flops 805306368 | bytes 3276800 | tf_op jit(solution)/shard_map/dot_general | solution.py:34
  57.5 0.0 reduce-scatter.5.cloned.1.call-update
  57.5 29.8 %reduce-scatter.5.cloned.1.call-done = f32[128,256]{1,0:T(8,128)} async-done(((f32[128,2048]{1,0:T(8,128)}), f32[128,256]{1,0:T(8,128)}) %reduce-scatter.5.cloned.1.call-update) | async-done | bytes 131088 | tf_op jit(solution)/shard_map/reduce_scatter | solution.py:37
  87.3 3.5 %collective-permute-start.1 = (f32[128,256]{1,0:T(8,128)}, f32[128,256]{1,0:T(8,128)S(1)}, u32[]{:S(2)}, u32[]{:S(2)}) collective-permute-start(f32[128,256]{1,0:T(8,128)} %reduce-scatter.5.cloned.1.call-done), channel_id=1, source_target_pairs={{0,8},{8,16},{16,24},{1,9},{9,17},{17,25},{2,10},{10,18},{18,26},{... | collective-permute-start | bytes 393224 | tf_op jit(solution)/shard_map/ppermute | solution.py:10
  90.9 0.7 pad_maximum_fusion
  91.6 3.7 %collective-permute-done.1 = f32[128,256]{1,0:T(8,128)S(1)} collective-permute-done((f32[128,256]{1,0:T(8,128)}, f32[128,256]{1,0:T(8,128)S(1)}, u32[]{:S(2)}, u32[]{:S(2)}) %collective-permute-start.1) | collective-permute-done | bytes 131104 | tf_op jit(solution)/shard_map/ppermute | solution.py:10
  95.3 0.7 copy.11
  (1 shorter events, 0.0 us)
Async XLA Ops:
  7.2 3.6 %copy-start = (f32[256,256]{1,0:T(8,128)S(1)}, f32[256,256]{1,0:T(8,128)}, u32[]{:S(2)}) copy-start(f32[256,256]{1,0:T(8,128)} %param.7) | copy-start | bytes 786436
  7.2 1.6 %copy-start.4 = (s32[1,8]{1,0:T(1,128)S(1)}, s32[1,8]{1,0:T(1,128)}, u32[]{:S(2)}) copy-start(s32[1,8]{1,0:T(1,128)} %param.9) | copy-start | bytes 100
  7.2 1.6 %copy-start.3 = (s32[1,8]{1,0:T(1,128)S(1)}, s32[1,8]{1,0:T(1,128)}, u32[]{:S(2)}) copy-start(s32[1,8]{1,0:T(1,128)} %param.10) | copy-start | bytes 100
  7.2 39.9 %reduce-scatter.3.cloned.1.call-start = ((), (), s32[]{:S(2)}) async-start(), calls=%async_computation.2 | async-start | bytes 1179648 | tf_op jit(solution)/shard_map/reduce_scatter | solution.py:37
  9.8 1.0 copy-start.1
  9.9 1.0 copy-start.2
  13.4 74.0 %reduce-scatter.5.cloned.1.call-start = ((), (), s32[]{:S(2)}) async-start(), calls=%async_computation.3 | async-start | bytes 1179648 | tf_op jit(solution)/shard_map/reduce_scatter | solution.py:37
  47.1 8.0 %collective-permute-start = (f32[128,256]{1,0:T(8,128)}, f32[128,256]{1,0:T(8,128)S(1)}, u32[]{:S(2)}, u32[]{:S(2)}) collective-permute-start(f32[128,256]{1,0:T(8,128)} %reduce-scatter.3.cloned.1.call-done), channel_id=1, source_target_pairs={{0,8},{8,16},{16,24},{1,9},{9,17},{17,25},{2,10},{10,18},{18,26},{... | collective-permute-start | bytes 393224 | tf_op jit(solution)/shard_map/ppermute | solution.py:10
  87.3 8.0 %collective-permute-start.1 = (f32[128,256]{1,0:T(8,128)}, f32[128,256]{1,0:T(8,128)S(1)}, u32[]{:S(2)}, u32[]{:S(2)}) collective-permute-start(f32[128,256]{1,0:T(8,128)} %reduce-scatter.5.cloned.1.call-done), channel_id=1, source_target_pairs={{0,8},{8,16},{16,24},{1,9},{9,17},{17,25},{2,10},{10,18},{18,26},{... | collective-permute-start | bytes 393224 | tf_op jit(solution)/shard_map/ppermute | solution.py:10
Sparse Core Ops, SparseCore 0:
  13.5 33.5 reduce-scatter.2
  57.6 29.6 reduce-scatter.4
where the time goes:
time: 103 us
  waiting for transfers between devices  71.7 us (70%)
  between operations  14.2 us (14%)
  starting transfers between devices  6.99 us (7%)
  matrix products  5.97 us (6%)
  local copies, waits for them, and re-layouts  3.18 us (3%)
    reduce_scatter x2, waiting for transfers between devices, shards(): summed = lax.psum_scatter(routed, 'own', scatter_dimension=1, tiled=True)  63.4 us
    ppermute x2, waiting for transfers between devices, passed_along(): return lax.ppermute(value, axis, pairs)  8.27 us
    ppermute x2, starting transfers between devices, passed_along(): return lax.ppermute(value, axis, pairs)  6.91 us
    dot_general x2, matrix products, shards(): jnp.dot(solved, routed_tiles, precision=highest, preferred_element_type=j...  4.41 us
    unnamed x13, local copies, waits for them, and re-layouts  3.18 us
  transfers between devices with their start and end apart: 4, of which 4 were waited for; matrix products, arithmetic and copies ran while one was open for 1% of the time, Pallas kernels for 0%

commit v1 on v0

v1 whole, which is shorter than its diff:
```python
import functools

import jax
import jax.numpy as jnp
from jax import lax
from jax.experimental import pallas as pl
from jax.experimental.pallas import tpu as pltpu
from jax.sharding import PartitionSpec as P

MESH = pl.DeviceIdType.MESH
GROUPS = 2


def halves(x):
    high = x.astype(jnp.bfloat16)
    low = (x - high.astype(jnp.float32)).astype(jnp.bfloat16)
    return high, low


def kernel(
    sections, chips, groups, rs_hbm, d_hbm, f_hbm, st_ref, an_ref, ca_hbm, sol_ref, co_ref,
    rs, d, f, ca, part, other, up_in, down_in, hop_in,
    in_sem, xs, xr, us, ur, ds, dr, hs, hr,
):
    ticks, chain, block = rs.shape
    rows = chain // groups
    slots = an_ref.shape[1]
    sec, own = lax.axis_index("sec"), lax.axis_index("own")
    z, c = own // 2, own % 2
    loads = [
        pltpu.make_async_copy(src, dst, in_sem.at[i])
        for i, (src, dst) in enumerate(((rs_hbm, rs), (ca_hbm, ca), (d_hbm, d)))
    ]
    loads += [
        pltpu.make_async_copy(f_hbm.at[:, pl.ds(a * block, block)], f.at[a], in_sem.at[3 + a])
        for a in range(slots)
    ]
    for load in loads:
        load.start()

    partner = own + 1 - 2 * c
    greets = [
        (None, {"own": partner}),
        (z > 0, {"own": own - 2}),
        (z < chips - 1, {"own": own + 2}),
        (sec > 0, {"sec": sec - 1}),
        (sec < sections - 1, {"sec": sec + 1}),
    ]
    barrier = pltpu.get_barrier_semaphore()
    for there, device in greets:
        def greet(device=device):
            pl.semaphore_signal(barrier, inc=1, device_id=device, device_id_type=MESH)
        if there is None:
            greet()
        else:
            pl.when(there)(greet)
    peers = 1
    for there, _ in greets[1:]:
        peers = peers + there.astype(jnp.int32)
    pl.semaphore_wait(barrier, peers)

    active = sec < sections - 1

    def remote(src, dst, send, recv, device):
        return pltpu.make_async_remote_copy(
            src_ref=src, dst_ref=dst, send_sem=send, recv_sem=recv,
            device_id=device, device_id_type=MESH,
        )

    def swap(n, dst):
        return remote(part.at[n, 1 - c, dst], other.at[n, dst], xs.at[n, dst], xr.at[n, dst], {"own": partner})

    def up(n, dst):
        return remote(part.at[n, c, dst], up_in.at[n, dst], us.at[n, dst], ur.at[n, dst], {"own": own + 2})

    def down(n, dst):
        return remote(part.at[n, c, dst], down_in.at[n, dst], ds.at[n, dst], dr.at[n, dst], {"own": own - 2})

    def hop(n):
        return remote(part.at[n, c, z], hop_in.at[n], hs.at[n], hr.at[n], {"sec": sec + 1})

    order = []
    for i in range(chips):
        order.append(chips - 1 - i // 2 if i % 2 == 0 else i // 2)

    def slot_of(j):
        found, present = jnp.int32(0), jnp.int32(0)
        for a in range(slots):
            here = (an_ref[0, a] == j).astype(jnp.int32)
            found = found + here * a
            present = present + here * st_ref[0, a]
        return jnp.minimum(found, slots - 1), present.astype(jnp.float32)

    where = {}
    for side in (0, 1):
        for dst in order:
            where[side, dst] = slot_of(2 * dst + (1 - c if side == 0 else c))

    for load in loads[:3]:
        load.wait()
    d_high, d_low = halves(d[...])

    def start(n):
        t, g = divmod(n, groups)
        span = pl.ds(g * rows, rows)
        if t == 0:
            x = rs[t, span, :] - ca[span, :]
        else:
            @pl.when(sec > 0)
            def _():
                hop(n - groups).wait_recv()
                rs[t, span, :] = rs[t, span, :] - hop_in[n - groups]
            x = rs[t, span, :]
        x_high, x_low = halves(x)
        both = jnp.dot(
            jnp.concatenate([x_high, x_low], axis=0), d_high, preferred_element_type=jnp.float32
        )
        solved = both[:rows] + both[rows:] + jnp.dot(x_high, d_low, preferred_element_type=jnp.float32)
        sol_ref[t, span, :] = solved
        if n == 0:
            for load in loads[3:]:
                load.wait()

        @pl.when(active)
        def _():
            stacked = jnp.concatenate(halves(solved), axis=0)
            for side in (0, 1):
                for dst in order:
                    at, there = where[side, dst]
                    out = jnp.dot(
                        stacked, f[at], preferred_element_type=jnp.float32
                    )
                    part[n, 1 - c if side == 0 else c, dst] = (out[:rows] + out[rows:]) * there
                    if side == 0:
                        swap(n, dst).start()

    def forward(n, tau):
        @pl.when(active & (tau >= z))
        def _():
            dst = chips - 1 - tau + z
            swap(n, dst).wait_recv()

            @pl.when(z > 0)
            def _():
                up(n, dst).wait_recv()
                part[n, c, dst] = part[n, c, dst] + other[n, dst] + up_in[n, dst]

            @pl.when(z == 0)
            def _():
                part[n, c, dst] = part[n, c, dst] + other[n, dst]

            up(n, dst).start()

        @pl.when(active & (tau >= chips - 1 - z))
        def _():
            dst = tau - (chips - 1 - z)
            swap(n, dst).wait_recv()

            @pl.when(z < chips - 1)
            def _():
                down(n, dst).wait_recv()
                part[n, c, dst] = part[n, c, dst] + other[n, dst] + down_in[n, dst]

            @pl.when(z == chips - 1)
            def _():
                part[n, c, dst] = part[n, c, dst] + other[n, dst]

            down(n, dst).start()

    def finish(n):
        @pl.when(active)
        def _():
            swap(n, z).wait_recv()
            part[n, c, z] = part[n, c, z] + other[n, z]

            @pl.when(z > 0)
            def _():
                up(n, z).wait_recv()
                part[n, c, z] = part[n, c, z] + up_in[n, z]

            @pl.when(z < chips - 1)
            def _():
                down(n, z).wait_recv()
                part[n, c, z] = part[n, c, z] + down_in[n, z]

            hop(n).start()

    steps = ticks * groups
    for n in range(steps):
        if n >= 1 and groups == 1:
            finish(n - 1)
        start(n)
        forward(n, 0)
        if n >= 1 and groups > 1:
            finish(n - 1)
        for tau in range(1, chips - 1):
            forward(n, tau)
    finish(steps - 1)

    @pl.when(sec == 0)
    def _():
        co_ref[...] = jnp.zeros_like(co_ref)

    for g in range(groups):
        @pl.when(sec > 0)
        def _(g=g):
            n = (ticks - 1) * groups + g
            hop(n).wait_recv()
            co_ref[pl.ds(g * rows, rows), :] = hop_in[n]

    @pl.when(active)
    def _():
        for n in range(steps):
            hop(n).wait_send()
            for dst in range(chips):
                swap(n, dst).wait_send()
                pl.when(z < dst)(lambda n=n, dst=dst: up(n, dst).wait_send())
                pl.when(z > dst)(lambda n=n, dst=dst: down(n, dst).wait_send())


def solution(mesh):
    sections, owners = mesh.shape["sec"], mesh.shape["own"]
    chips = owners // 2

    def shards(right_sides, inv_diag, factor_tiles, structure, ancestor, carried):
        ticks, chain, block = right_sides.shape
        slots = structure.shape[1]
        steps, rows = ticks * GROUPS, chain // GROUPS
        flag = pltpu.SemaphoreType.DMA
        f32 = jnp.float32
        hbm = pl.BlockSpec(memory_space=pl.ANY)
        smem = pl.BlockSpec(memory_space=pltpu.SMEM)
        vmem = pl.BlockSpec(memory_space=pltpu.VMEM)
        return pl.pallas_call(
            functools.partial(kernel, sections, chips, GROUPS),
            out_shape=(
                jax.ShapeDtypeStruct(right_sides.shape, f32),
                jax.ShapeDtypeStruct(carried.shape, f32),
            ),
            in_specs=[hbm, hbm, hbm, smem, smem, hbm],
            out_specs=(vmem, vmem),
            scratch_shapes=[
                pltpu.VMEM(right_sides.shape, f32),
                pltpu.VMEM(inv_diag.shape, f32),
                pltpu.VMEM((slots, block, block), factor_tiles.dtype),
                pltpu.VMEM(carried.shape, f32),
                pltpu.VMEM((steps, 2, chips, rows, block), f32),
                pltpu.VMEM((steps, chips, rows, block), f32),
                pltpu.VMEM((steps, chips, rows, block), f32),
                pltpu.VMEM((steps, chips, rows, block), f32),
                pltpu.VMEM((steps, rows, block), f32),
                flag((3 + slots,)),
                *[flag((steps, chips))] * 6,
                *[flag((steps,))] * 2,
            ],
            compiler_params=pltpu.CompilerParams(
                collective_id=0, has_side_effects=True, vmem_limit_bytes=40 * 1024 * 1024
            ),
        )(right_sides, inv_diag, factor_tiles, structure, ancestor, carried)

    in_specs = (
        P(None, None, ("sec", "own")),
        P(("sec", "own"), None),
        P(("sec", "own"), None),
        P(("sec", "own"), None),
        P("sec", None),
        P(None, ("sec", "own")),
    )
    out_specs = (P(None, None, ("sec", "own")), P(None, ("sec", "own")))
    return jax.shard_map(shards, mesh=mesh, in_specs=in_specs, out_specs=out_specs, check_vma=False)
```

time: 103 us -> 49.4 us (0.48)
  the two profiles are of different devices: /device:TPU:4 before, /device:TPU:14 now
where the time goes in v1:
time: 49.4 us; the launch traced here: 49.1 us
  Pallas kernels  41.8 us (85%)
  local copies, waits for them, and re-layouts  6.69 us (14%)
  between operations  0.65 us (1%)
    pallas_call x1, Pallas kernels, shards(): pl.pallas_call(functools.partial(kernel, sections, chips, GROUPS), out_sh...  41.8 us
    unnamed x14, local copies, waits for them, and re-layouts  6.69 us

profile of v1, /device:TPU:14, one launch (start us, length us, event | category | flops | bytes accessed | tf_op | source)
XLA Modules:
  0.0 49.1 jit_solution(8109435711469188063)
XLA Ops:
  0.6 0.0 copy-start
  0.6 1.2 %copy-done = bf16[256,2048]{1,0:T(8,128)(2,1)S(1)} copy-done((bf16[256,2048]{1,0:T(8,128)(2,1)S(1)}, bf16[256,2048]{1,0:T(8,128)(2,1)}, u32[]{:S(2)}) %copy-start) | copy-done | bytes 1048600
  1.9 0.0 copy-start.1
  1.9 0.9 %copy-done.1 = f32[2,128,256]{2,1,0:T(8,128)S(1)} copy-done((f32[2,128,256]{2,1,0:T(8,128)S(1)}, f32[2,128,256]{2,1,0:T(8,128)}, u32[]{:S(2)}) %copy-start.1) | copy-done | bytes 262168
  2.8 0.0 copy-start.2
  2.8 0.9 %copy-done.2 = f32[256,256]{1,0:T(8,128)S(1)} copy-done((f32[256,256]{1,0:T(8,128)S(1)}, f32[256,256]{1,0:T(8,128)}, u32[]{:S(2)}) %copy-start.2) | copy-done | bytes 262168
  3.8 0.0 copy-start.3
  3.8 0.9 %copy-done.3 = f32[128,256]{1,0:T(8,128)S(1)} copy-done((f32[128,256]{1,0:T(8,128)S(1)}, f32[128,256]{1,0:T(8,128)}, u32[]{:S(2)}) %copy-start.3) | copy-done | bytes 131096
  4.7 0.0 copy-start.4
  4.7 0.7 %copy-done.4 = s32[1,8]{1,0:T(1,128)S(1)} copy-done((s32[1,8]{1,0:T(1,128)S(1)}, s32[1,8]{1,0:T(1,128)}, u32[]{:S(2)}) %copy-start.4) | copy-done | bytes 56
  5.3 0.0 copy-start.5
  5.3 0.7 %copy-done.5 = s32[1,8]{1,0:T(1,128)S(1)} copy-done((s32[1,8]{1,0:T(1,128)S(1)}, s32[1,8]{1,0:T(1,128)}, u32[]{:S(2)}) %copy-start.5) | copy-done | bytes 56
  6.0 41.8 %shard_map.77 = (f32[2,128,256]{2,1,0:T(8,128)S(1)}, f32[128,256]{1,0:T(8,128)S(1)}) custom-call(f32[2,128,256]{2,1,0:T(8,128)S(1)} %copy-done.1, f32[256,256]{1,0:T(8,128)S(1)} %copy-done.2, bf16[256,2048]{1,0:T(8,128)(2,1)S(1)} %copy-done, s32[1,8]{1,0:T(1,128)S(1)} %copy-done.4, s32[1,8]{1,0:T(1,128)S(1)} %copy-done.5, f32[128,256]{1,0:T(8,128)S(1)} %copy-done.3), custom_call_target="tpu_custom_call" | custom-call | tf_op jit(solution)/shard_map/pallas_call | solution.py:234
  47.8 0.7 %copy.10 = f32[2,128,256]{2,1,0:T(8,128)} copy(f32[2,128,256]{2,1,0:T(8,128)S(1)} %get-tuple-element.4) | data formatting | bytes 524288
  48.5 0.7 %copy.11 = f32[128,256]{1,0:T(8,128)} copy(f32[128,256]{1,0:T(8,128)S(1)} %get-tuple-element.5) | data formatting | bytes 262144
Async XLA Ops:
  0.6 1.2 %copy-start = (bf16[256,2048]{1,0:T(8,128)(2,1)S(1)}, bf16[256,2048]{1,0:T(8,128)(2,1)}, u32[]{:S(2)}) copy-start(bf16[256,2048]{1,0:T(8,128)(2,1)} %f_hbm.1) | copy-start | bytes 3145732
  1.9 0.9 %copy-start.1 = (f32[2,128,256]{2,1,0:T(8,128)S(1)}, f32[2,128,256]{2,1,0:T(8,128)}, u32[]{:S(2)}) copy-start(f32[2,128,256]{2,1,0:T(8,128)} %rs_hbm.1) | copy-start | bytes 786436
  2.8 0.9 %copy-start.2 = (f32[256,256]{1,0:T(8,128)S(1)}, f32[256,256]{1,0:T(8,128)}, u32[]{:S(2)}) copy-start(f32[256,256]{1,0:T(8,128)} %d_hbm.1) | copy-start | bytes 786436
  3.8 0.9 %copy-start.3 = (f32[128,256]{1,0:T(8,128)S(1)}, f32[128,256]{1,0:T(8,128)}, u32[]{:S(2)}) copy-start(f32[128,256]{1,0:T(8,128)} %ca_hbm.1) | copy-start | bytes 393220
  4.7 0.7 %copy-start.4 = (s32[1,8]{1,0:T(1,128)S(1)}, s32[1,8]{1,0:T(1,128)}, u32[]{:S(2)}) copy-start(s32[1,8]{1,0:T(1,128)} %st_ref.1) | copy-start | bytes 100
  5.3 0.7 %copy-start.5 = (s32[1,8]{1,0:T(1,128)S(1)}, s32[1,8]{1,0:T(1,128)}, u32[]{:S(2)}) copy-start(s32[1,8]{1,0:T(1,128)} %an_ref.1) | copy-start | bytes 100

commit v2 on v1

--- a/solution.py
+++ b/solution.py
@@ -9,6 +9,7 @@
 
 MESH = pl.DeviceIdType.MESH
 GROUPS = 2
+LAG = 0.1
 
 
 def halves(x):
@@ -186,16 +187,18 @@
             hop(n).start()
 
     steps = ticks * groups
+    waves = chips - 1
+    period = waves * groups + 1 + min(groups - 1, 2) + 0.5
+    plan = []
     for n in range(steps):
-        if n >= 1 and groups == 1:
-            finish(n - 1)
-        start(n)
-        forward(n, 0)
-        if n >= 1 and groups > 1:
-            finish(n - 1)
-        for tau in range(1, chips - 1):
-            forward(n, tau)
-    finish(steps - 1)
+        t, g = divmod(n, groups)
+        first = t * period + g
+        plan.append((first, functools.partial(start, n)))
+        for tau in range(waves):
+            plan.append((first + LAG + tau * groups, functools.partial(forward, n, tau)))
+        plan.append((first + LAG + waves * groups, functools.partial(finish, n)))
+    for _, event in sorted(plan, key=lambda entry: entry[0]):
+        event()
 
     @pl.when(sec == 0)
     def _():
@@ -254,7 +257,7 @@
                 *[flag((steps,))] * 2,
             ],
             compiler_params=pltpu.CompilerParams(
-                collective_id=0, has_side_effects=True, vmem_limit_bytes=40 * 1024 * 1024
+                collective_id=0, has_side_effects=True, vmem_limit_bytes=62 * 1024 * 1024
             ),
         )(right_sides, inv_diag, factor_tiles, structure, ancestor, carried)
 

time: 49.4 us -> 41.1 us (0.83)
  the two profiles are of different devices: /device:TPU:14 before, /device:TPU:4 now
where the time goes in v2:
time: 41.1 us; the launch traced here: 40.5 us
  Pallas kernels  37.5 us (91%)
  local copies, waits for them, and re-layouts  2.36 us (6%)
  between operations  0.65 us (2%)
    pallas_call x1, Pallas kernels, shards(): pl.pallas_call(functools.partial(kernel, sections, chips, GROUPS), out_sh...  37.5 us
    unnamed x4, local copies, waits for them, and re-layouts  2.36 us

profile of v2, /device:TPU:4, one launch (start us, length us, event | category | flops | bytes accessed | tf_op | source)
XLA Modules:
  0.0 40.5 jit_solution(9776270681730114095)
XLA Ops:
  0.6 37.5 %shard_map.77 = (f32[2,128,256]{2,1,0:T(8,128)}, f32[128,256]{1,0:T(8,128)}) custom-call(f32[2,128,256]{2,1,0:T(8,128)} %rs_hbm.1, f32[256,256]{1,0:T(8,128)} %d_hbm.1, bf16[256,2048]{1,0:T(8,128)(2,1)} %f_hbm.1, s32[1,8]{1,0:T(1,128)} %st_ref.1, s32[1,8]{1,0:T(1,128)} %an_ref.1, f32[128,256]{1,0:T(8,128)} %ca_hbm.1), custom_call_target="tpu_custom_call" | custom-call | tf_op jit(solution)/shard_map/pallas_call | solution.py:237
  38.1 0.0 copy-start
  38.2 1.7 %copy.10 = f32[2,128,256]{2,1,0:T(8,128)} copy(f32[2,128,256]{2,1,0:T(8,128)} %get-tuple-element.4) | data formatting | bytes 524288
  39.9 0.0 copy-done
  39.9 0.7 %copy.11 = f32[128,256]{1,0:T(8,128)} copy(f32[128,256]{1,0:T(8,128)S(1)} %copy-done) | data formatting | bytes 262144
Async XLA Ops:
  38.1 1.7 %copy-start = (f32[128,256]{1,0:T(8,128)S(1)}, f32[128,256]{1,0:T(8,128)}, u32[]{:S(2)}) copy-start(f32[128,256]{1,0:T(8,128)} %get-tuple-element.5) | copy-start | bytes 393220
